TPU v7x, 128 devices: a whole 4x4x4 slice. The times are simulated.
128 devices in a mesh: row: 16 (over x, y_hi, core), col: 8 (over z, y_lo).
Axes of the slice: x: 4, y: 4 (y_hi: 2, y_lo: 2; y = y_hi * 2 + y_lo), z: 4, core: 2. Of those that a mesh axis runs over, the one named last changes fastest.
Arguments:
- features: bfloat16 [131072, 128], P(('row', 'col')), may hold values from -6 to 6
- weight: bfloat16 [128, 128], replicated, may hold values from -0.5 to 0.5
- layer_bias: float32 [128], replicated, may hold values from -3 to 3
- cotangent: bfloat16 [131072, 128], P(('col', 'row')), may hold values from -6 to 6
- tile_out: int32 [16, 8, 128], P('row', 'col'), may hold values from 0 to 63
- tile_in: int32 [16, 8, 128], P('row', 'col'), may hold values from 0 to 31
- tile_vals: bfloat16 [16, 8, 128, 256, 256], P('row', 'col'), may hold values from -0.09375 to 0.09375
- tile_count: int32 [16, 8], P('row', 'col'), may hold values from 1 to 128, as said below
Outputs:
- hidden_out: bfloat16 [131072, 128], P(('col', 'row'))
- feature_grad: bfloat16 [131072, 128], P(('row', 'col'))
- weight_grad: float32 [128, 128], replicated
- bias_grad: float32 [128], replicated
Inputs may be any that keep to these rules, and one draw needn't show every extreme that they name: `tile_count`: live slots of each grid block; some grid block has exactly 128 in every draw.
All inputs are finite; a program needn't handle non-finite values.
Results may differ from a plain program's by a relative error of at most 0.025.
Values may be sent and summed in bfloat16 or wider, within the bound.
No kernel may reach another device: no remote copies, remote signals or barrier semaphores. Data moves between devices by JAX's collectives and lax.ppermute only.
A program may use at most 192 MiB of HBM per device.

v0:
```python
import math
import jax
import jax.numpy as jnp
from jax import lax
from jax.sharding import PartitionSpec as P

gelu_coef = 0.7978845608
cube_coef = 0.044715


def gelu_tanh(inputs):
    inner = jnp.tanh(gelu_coef * (inputs + cube_coef * inputs * inputs * inputs))
    return 0.5 * inputs * (1.0 + inner)


def gelu_slope(inputs):
    inner = jnp.tanh(gelu_coef * (inputs + cube_coef * inputs * inputs * inputs))
    return 0.5 * (1.0 + inner) + 0.5 * inputs * (1.0 - inner * inner) * gelu_coef * (
        1.0 + 3.0 * cube_coef * inputs * inputs
    )


def tile_sums(products, targets, live_mask, target_tiles):
    masked = products * live_mask[:, None, None]
    summed = (
        jnp.zeros((target_tiles, products.shape[1], products.shape[2]), jnp.float32)
        .at[targets]
        .add(masked)
    )
    return summed.reshape(target_tiles * products.shape[1], products.shape[2])


def local(features, weight, layer_bias, cotangent, tile_out, tile_in, tile_vals, tile_count):
    tile_size = tile_vals.shape[-1]
    slot_count = tile_vals.shape[2]
    node_rows = features.shape[0]
    feat_count = features.shape[1]
    rows_axis = lax.axis_size("row")
    cols_axis = lax.axis_size("col")
    target_tiles = rows_axis * node_rows // tile_size
    source_tiles = cols_axis * node_rows // tile_size
    out_index = tile_out[0, 0]
    in_index = tile_in[0, 0]
    values = tile_vals[0, 0]
    live_mask = (jnp.arange(slot_count, dtype=jnp.int32) < tile_count[0, 0]).astype(jnp.float32)
    source_rows = lax.all_gather(features, "col", axis=0, tiled=True)
    picked = jnp.take(source_rows.reshape(source_tiles, tile_size, feat_count), in_index, axis=0)
    products = jnp.einsum("tab,tbf->taf", values, picked, preferred_element_type=jnp.float32)
    partial_value = tile_sums(products, out_index, live_mask, target_tiles).astype(jnp.bfloat16)
    own_agg = (
        lax.psum_scatter(partial_value, "row", scatter_dimension=0, tiled=True)
        .astype(jnp.float32)
        .astype(jnp.bfloat16)
    )
    preact = jnp.dot(own_agg, weight, preferred_element_type=jnp.float32) + layer_bias
    hidden_out = gelu_tanh(preact).astype(jnp.bfloat16)
    own_grad = (cotangent.astype(jnp.float32) * gelu_slope(preact)).astype(jnp.bfloat16)
    grad_local = jnp.dot(own_grad, weight.T, preferred_element_type=jnp.float32).astype(
        jnp.bfloat16
    )
    target_grad = lax.all_gather(grad_local, "row", axis=0, tiled=True)
    weight_local = lax.dot_general(
        own_agg, own_grad, (((0,), (0,)), ((), ())), preferred_element_type=jnp.float32
    )
    bias_local = jnp.sum(own_grad.astype(jnp.float32), axis=0)
    weight_total, bias_total = lax.psum((weight_local, bias_local), ("row", "col"))
    norm_scale = 1.0 / math.sqrt(node_rows * rows_axis * cols_axis)
    weight_grad = weight_total * norm_scale
    bias_grad = bias_total * norm_scale
    picked_grad = jnp.take(
        target_grad.reshape(target_tiles, tile_size, feat_count), out_index, axis=0
    )
    back_products = jnp.einsum(
        "tab,taf->tbf", values, picked_grad, preferred_element_type=jnp.float32
    )
    back_partial = tile_sums(back_products, in_index, live_mask, source_tiles).astype(jnp.bfloat16)
    feature_grad = (
        lax.psum_scatter(back_partial, "col", scatter_dimension=0, tiled=True)
        .astype(jnp.float32)
        .astype(jnp.bfloat16)
    )
    return (hidden_out, feature_grad, weight_grad, bias_grad)


def solution(mesh):
    in_specs = (
        P(("row", "col"), None),
        P(),
        P(),
        P(("col", "row"), None),
        P("row", "col", None),
        P("row", "col", None),
        P("row", "col", None, None, None),
        P("row", "col"),
    )
    out_specs = (P(("col", "row"), None), P(("row", "col"), None), P(), P())
    return jax.shard_map(local, mesh=mesh, in_specs=in_specs, out_specs=out_specs, check_vma=False)
```

profile of v0, /device:TPU:1, one launch (start us, length us, event | category | flops | bytes accessed | tf_op | source)
XLA Modules:
  0.0 496.3 jit_solution(11982166304795398902)
XLA Ops:
  7.2 0.0 copy-start
  7.2 0.0 all-gather.3.cloned.1.call-start
  7.2 0.7 all-gather.3.cloned.1.call-update
  7.9 0.0 reduce-scatter.3.cloned.1.call-start
  8.6 0.7 fusion.22
  9.3 0.7 fusion.21
  9.9 0.7 compare_convert_fusion
  10.6 54.4 %all-gather.3.cloned.1.call-done = bf16[8192,128]{1,0:T(8,128)(2,1)} async-done(((bf16[1024,128]{1,0:T(8,128)(2,1)}), bf16[8192,128]{1,0:T(8,128)(2,1)}) %all-gather.3.cloned.1.call-update) | async-done | bytes 2097168 | tf_op jit(solution)/shard_map/all_gather | solution.py:46
  65.0 8.2 %gather_fusion = bf16[128,256,128]{2,1,0:T(8,128)(2,1)} fusion(bf16[32,256,128]{2,1,0:T(8,128)(2,1)} %bitcast.37, s32[1024]{0:T(1024)S(1)} %pad_clamp_fusion.1), kind=kCustom, calls=%fused_computation | custom fusion | bytes 16777728 | tf_op jit(solution)/shard_map/jit(_take)/gather | solution.py:47
  73.2 17.5 %multiply_bitcast_fusion.1 = f32[128,256,128]{1,2,0:T(8,128)} fusion(bf16[1,1,128,256,256]{4,3,2,1,0:T(8,128)(2,1)} %param.14, f32[128]{0:T(128)S(1)} %get-tuple-element.7, bf16[128,256,128]{2,1,0:T(8,128)(2,1)} %gather_fusion, pred[128]{0:T(512)(128)(4,1)S(1)} %get-tuple-element.8), kind=kOutput, calls=%fused_computation.9 | convolution fusion | flops 2155872256 | bytes 41943680 | tf_op jit(solution)/shard_map/tab,tbf->taf/dot_general | solution.py:48
  90.7 17.4 %copy.15 = f32[128,256,128]{2,1,0:T(8,128)} copy(f32[128,256,128]{1,2,0:T(8,128)} %multiply_bitcast_fusion.1) | data formatting | bytes 33554432 | tf_op jit(solution)/shard_map/mul | solution.py:24
  108.1 4.2 broadcast_in_dim.29
  112.3 38.5 %scatter_fusion = f32[64,256,128]{2,1,0:T(8,128)} fusion(f32[64,256,128]{2,1,0:T(8,128)} %broadcast_in_dim.29, s32[128]{0:T(128)S(1)} %fusion.21, f32[128,256,128]{2,1,0:T(8,128)} %copy.15), kind=kCustom, calls=%fused_computation.2 | custom fusion | flops 4194304 | bytes 50332160 | tf_op jit(solution)/shard_map/scatter-add | solution.py:28
  150.8 0.0 copy-start.2
  150.8 0.0 copy-start.3
  150.8 0.0 copy-start.4
  150.8 6.1 %convert_element_type.39 = bf16[64,256,128]{2,1,0:T(8,128)(2,1)} convert(f32[64,256,128]{2,1,0:T(8,128)} %scatter_fusion) | non-fusion elementwise | flops 2097152 | bytes 12582912 | tf_op jit(solution)/shard_map/convert_element_type | solution.py:49
  156.9 0.0 reduce-scatter.3.cloned.1.call-update
  156.9 0.0 all-gather.5.cloned.1.call-start
  157.0 78.4 %reduce-scatter.3.cloned.1.call-done = bf16[1024,128]{1,0:T(8,128)(2,1)} async-done(((bf16[16384,128]{1,0:T(8,128)(2,1)}), bf16[1024,128]{1,0:T(8,128)(2,1)}) %reduce-scatter.3.cloned.1.call-update) | async-done | bytes 262160 | tf_op jit(solution)/shard_map/reduce_scatter | solution.py:51
  235.4 0.0 copy-done
  235.4 0.0 copy-done.2
  235.4 0.0 copy-done.3
  235.4 2.2 convert_reduce_fusion
  237.6 0.9 convolution_convert_fusion
  238.5 0.0 all-gather.5.cloned.1.call-update
  238.6 0.0 all-reduce.2.cloned.1.call-start
  238.6 0.0 copy-done.4
  238.7 1.9 fusion.26
  240.5 0.0 all-reduce.2.cloned.1.call-update
  240.5 0.2 reduce-scatter.5.cloned.1.call-start
  240.8 54.7 %all-gather.5.cloned.1.call-done = bf16[16384,128]{1,0:T(8,128)(2,1)} async-done(((bf16[1024,128]{1,0:T(8,128)(2,1)}), bf16[16384,128]{1,0:T(8,128)(2,1)}) %all-gather.5.cloned.1.call-update) | async-done | bytes 4194320 | tf_op jit(solution)/shard_map/all_gather | solution.py:61
  295.4 8.7 %gather_fusion.1 = bf16[128,256,128]{2,1,0:T(8,128)(2,1)} fusion(bf16[64,256,128]{2,1,0:T(8,128)(2,1)} %bitcast.38, s32[1024]{0:T(1024)S(1)} %pad_clamp_fusion), kind=kCustom, calls=%fused_computation.1 | custom fusion | bytes 16777728 | tf_op jit(solution)/shard_map/jit(_take)/gather | solution.py:70
  304.2 14.0 %multiply_bitcast_fusion = f32[128,256,128]{1,2,0:T(8,128)} fusion(bf16[1,1,128,256,256]{4,3,2,1,0:T(8,128)(2,1)} %param.14, bf16[128,256,128]{2,1,0:T(8,128)(2,1)} %gather_fusion.1, f32[128]{0:T(128)S(1)} %get-tuple-element.7, pred[128]{0:T(512)(128)(4,1)S(1)} %compare_and_fusion), kind=kOutput, calls=%fused_computation.8 | convolution fusion | flops 2155872256 | bytes 41943680 | tf_op jit(solution)/shard_map/tab,taf->tbf/dot_general | solution.py:73
  318.2 17.4 %copy.17 = f32[128,256,128]{2,1,0:T(8,128)} copy(f32[128,256,128]{1,2,0:T(8,128)} %multiply_bitcast_fusion) | data formatting | bytes 33554432 | tf_op jit(solution)/shard_map/mul | solution.py:24
  335.6 2.4 broadcast_in_dim.32
  338.0 0.0 copy-start.1
  338.0 37.9 %scatter_fusion.1 = f32[32,256,128]{2,1,0:T(8,128)} fusion(f32[32,256,128]{2,1,0:T(8,128)} %broadcast_in_dim.32, s32[128]{0:T(128)S(1)} %fusion.22, f32[128,256,128]{2,1,0:T(8,128)} %copy.17), kind=kCustom, calls=%fused_computation.3 | custom fusion | flops 4194304 | bytes 50332160 | tf_op jit(solution)/shard_map/scatter-add | solution.py:28
  376.0 3.9 convert_element_type.45
  379.9 0.0 reduce-scatter.5.cloned.1.call-update
  379.9 64.8 %psum.15 = f32[128]{0:T(128)S(1)} all-reduce(f32[128]{0:T(128)S(1)} %get-tuple-element.4), channel_id=1, replica_groups=mesh['row'=16,'col'=8] {'row','col'}, use_global_device_ids=true, to_apply=%region_6.7 | all-reduce | flops 128 | bytes 1024 | tf_op jit(solution)/shard_map/psum | solution.py:66
  444.7 0.5 broadcast_multiply_fusion.1
  445.2 0.0 all-reduce.2.cloned.1.call-done
  445.2 1.5 broadcast_multiply_fusion
  446.6 43.1 %reduce-scatter.5.cloned.1.call-done = bf16[1024,128]{1,0:T(8,128)(2,1)} async-done(((bf16[8192,128]{1,0:T(8,128)(2,1)}), bf16[1024,128]{1,0:T(8,128)(2,1)}) %reduce-scatter.5.cloned.1.call-update) | async-done | bytes 262160 | tf_op jit(solution)/shard_map/reduce_scatter | solution.py:78
  489.8 0.0 copy-done.1
  (3 shorter events, 0.0 us)
Async XLA Ops:
  7.2 228.2 %copy-start = (bf16[128,128]{1,0:T(8,128)(2,1)S(1)}, bf16[128,128]{1,0:T(8,128)(2,1)}, u32[]{:S(2)}) copy-start(bf16[128,128]{1,0:T(8,128)(2,1)} %param.9) | copy-start | bytes 98308
  7.2 57.8 %all-gather.3.cloned.1.call-start = ((), (), s32[]{:S(2)}) async-start(), calls=%async_computation.2 | async-start | bytes 2359296 | tf_op jit(solution)/shard_map/all_gather | solution.py:46
  7.9 227.5 %reduce-scatter.3.cloned.1.call-start = ((), (), s32[]{:S(2)}) async-start(), calls=%async_computation.3 | async-start | bytes 4456448 | tf_op jit(solution)/shard_map/reduce_scatter | solution.py:51
  150.8 84.6 %copy-start.2 = (bf16[1024,128]{1,0:T(8,128)(2,1)S(1)}, bf16[1024,128]{1,0:T(8,128)(2,1)}, u32[]{:S(2)}) copy-start(bf16[1024,128]{1,0:T(8,128)(2,1)} %param.11) | copy-start | bytes 786436
  150.8 84.6 %copy-start.3 = (f32[128]{0:T(128)S(1)}, f32[128]{0:T(128)}, u32[]{:S(2)}) copy-start(f32[128]{0:T(128)} %param.10) | copy-start | bytes 1540
  150.8 87.8 %copy-start.4 = (s32[1,1,128]{2,1,0:T(1,128)S(1)}, s32[1,1,128]{2,1,0:T(1,128)}, u32[]{:S(2)}) copy-start(s32[1,1,128]{2,1,0:T(1,128)} %param.12) | copy-start | bytes 1540
  156.9 138.5 %all-gather.5.cloned.1.call-start = ((), (), s32[]{:S(2)}) async-start(), calls=%async_computation.4 | async-start | bytes 4456448 | tf_op jit(solution)/shard_map/all_gather | solution.py:61
  238.6 206.6 %all-reduce.2.cloned.1.call-start = ((), (), s32[]{:S(2)}) async-start(), calls=%async_computation.6 | async-start | bytes 131072 | tf_op jit(solution)/shard_map/psum | solution.py:66
  240.5 249.3 %reduce-scatter.5.cloned.1.call-start = ((), (), s32[]{:S(2)}) async-start(), calls=%async_computation.5 | async-start | bytes 2359296 | tf_op jit(solution)/shard_map/reduce_scatter | solution.py:78
  338.0 151.8 %copy-start.1 = (bf16[128,128]{1,0:T(8,128)(2,1)S(1)}, bf16[128,128]{1,0:T(8,128)(2,1)}, u32[]{:S(2)}) copy-start(bf16[128,128]{1,0:T(8,128)(2,1)} %param.9) | copy-start | bytes 98308
Sparse Core Ops, SparseCore 0:
  9.7 55.3 all-gather.2
  157.0 78.2 reduce-scatter.2
  238.7 56.6 all-gather.4
  301.3 136.4 all-reduce.1
  440.6 49.1 reduce-scatter.4
where the time goes:
time: 497 us; the launch traced here: 496 us
  waiting for transfers between devices  231 us (46%)
  other arithmetic  90.4 us (18%)
  blocking collectives  64.8 us (13%)
  local copies, waits for them, and re-layouts  58.4 us (12%)
  matrix products  36.6 us (7%)
  between operations  14.5 us (3%)
    reduce_scatter x1, waiting for transfers between devices, local(): lax.psum_scatter(partial_value, 'row', scatter_dimension=0, tiled=True)  78.4 us
    scatter-add x2, other arithmetic, tile_sums(): summed = jnp.zeros((target_tiles, products.shape[1], products.shape[2]),...  76.4 us
    psum x1, blocking collectives, local(): lax.psum((weight_local, bias_local), ('row', 'col'))  64.8 us
    all_gather x1, waiting for transfers between devices, local(): target_grad = lax.all_gather(grad_local, 'row', axis=0, tiled=True)  54.7 us
    all_gather x1, waiting for transfers between devices, local(): source_rows = lax.all_gather(features, 'col', axis=0, tiled=True)  54.4 us
    reduce_scatter x1, waiting for transfers between devices, local(): lax.psum_scatter(back_partial, 'col', scatter_dimension=0, tiled=True)  43.1 us
    mul x2, local copies, waits for them, and re-layouts, tile_sums(): masked = products * live_mask[:, None, None]  34.8 us
    dot_general x1, matrix products, local(): jnp.einsum('tab,tbf->taf', values, picked, preferred_element_type=jnp.flo...  17.5 us
  transfers between devices with their start and end apart: 5, of which 4 were waited for; matrix products, arithmetic and copies ran while one was open for 18% of the time, Pallas kernels for 0%

commit v1 on v0

--- a/solution.py
+++ b/solution.py
@@ -43,7 +43,9 @@
     in_index = tile_in[0, 0]
     values = tile_vals[0, 0]
     live_mask = (jnp.arange(slot_count, dtype=jnp.int32) < tile_count[0, 0]).astype(jnp.float32)
-    source_rows = lax.all_gather(features, "col", axis=0, tiled=True)
+    source_rows = jnp.concatenate(
+        lax.all_to_all(jnp.stack([features] * lax.axis_size("col")), "col", 0, 0), axis=0
+    )
     picked = jnp.take(source_rows.reshape(source_tiles, tile_size, feat_count), in_index, axis=0)
     products = jnp.einsum("tab,tbf->taf", values, picked, preferred_element_type=jnp.float32)
     partial_value = tile_sums(products, out_index, live_mask, target_tiles).astype(jnp.bfloat16)

time: 497 us -> 475 us (0.956)
  waiting for transfers between devices: 231 us -> 201 us
  starting transfers between devices: 0.38 us -> 7.22 us
    all_gather x1 -> x0, waiting for transfers between devices: 54.4 us -> none  [local(): source_rows = lax.all_gather(features, 'col', axis=0, tiled=True)]
    all_to_all x0 -> x1, waiting for transfers between devices: none -> 23.4 us  [local(): lax.all_to_all(jnp.stack([features] * lax.axis_size('col')), 'col', 0, 0)]
    all_to_all x0 -> x1, starting transfers between devices: none -> 6.88 us  [local(): lax.all_to_all(jnp.stack([features] * lax.axis_size('col')), 'col', 0, 0)]
  transfers between devices with their start and end apart: 5 -> 5, of which waited for: 4 -> 4; matrix products, arithmetic and copies ran while one was open for 18% -> 19% of each run, Pallas kernels for 0% -> 0%
where the time goes in v1:
time: 475 us; the launch traced here: 474 us
  waiting for transfers between devices  201 us (42%)
  other arithmetic  90.4 us (19%)
  blocking collectives  64.8 us (14%)
  local copies, waits for them, and re-layouts  59.4 us (13%)
  matrix products  36.6 us (8%)
  between operations  14.5 us (3%)
  starting transfers between devices  7.22 us (2%)
    reduce_scatter x1, waiting for transfers between devices, local(): lax.psum_scatter(partial_value, 'row', scatter_dimension=0, tiled=True)  80 us
    scatter-add x2, other arithmetic, tile_sums(): summed = jnp.zeros((target_tiles, products.shape[1], products.shape[2]),...  76.4 us
    psum x1, blocking collectives, local(): lax.psum((weight_local, bias_local), ('row', 'col'))  64.8 us
    all_gather x1, waiting for transfers between devices, local(): target_grad = lax.all_gather(grad_local, 'row', axis=0, tiled=True)  54.7 us
    reduce_scatter x1, waiting for transfers between devices, local(): lax.psum_scatter(back_partial, 'col', scatter_dimension=0, tiled=True)  43.3 us
    mul x2, local copies, waits for them, and re-layouts, tile_sums(): masked = products * live_mask[:, None, None]  34.8 us
    all_to_all x1, waiting for transfers between devices, local(): lax.all_to_all(jnp.stack([features] * lax.axis_size('col')), 'col', 0, 0)  23.4 us
    dot_general x1, matrix products, local(): jnp.einsum('tab,tbf->taf', values, picked, preferred_element_type=jnp.flo...  17.5 us
  transfers between devices with their start and end apart: 5, of which 4 were waited for; matrix products, arithmetic and copies ran while one was open for 19% of the time, Pallas kernels for 0%

profile of v1, /device:TPU:1, one launch (start us, length us, event | category | flops | bytes accessed | tf_op | source)
XLA Modules:
  0.0 474.2 jit_solution(1333036969258003019)
XLA Ops:
  7.2 0.0 copy-start
  7.2 2.6 stack.2
  9.8 6.9 %all-to-all-start = ((bf16[8,1024,128]{2,1,0:T(8,128)(2,1)}), bf16[8,1024,128]{2,1,0:T(8,128)(2,1)S(1)}, u32[]{:S(2)}, u32[]{:S(2)}) async-start(bf16[8,1024,128]{2,1,0:T(8,128)(2,1)} %stack.2), calls=%async_computation | async-start | bytes 4194304 | tf_op jit(solution)/shard_map/all_to_all | solution.py:47
  16.6 0.0 reduce-scatter.3.cloned.1.call-start
  17.3 0.7 fusion.22
  18.0 0.7 fusion.21
  18.6 0.7 compare_convert_fusion
  19.3 23.4 %all-to-all-done = bf16[8,1024,128]{2,1,0:T(8,128)(2,1)S(1)} async-done(((bf16[8,1024,128]{2,1,0:T(8,128)(2,1)}), bf16[8,1024,128]{2,1,0:T(8,128)(2,1)S(1)}, u32[]{:S(2)}, u32[]{:S(2)}) %all-to-all-start) | async-done | bytes 2097184 | tf_op jit(solution)/shard_map/all_to_all | solution.py:47
  42.7 6.6 %gather_fusion = bf16[128,256,128]{2,1,0:T(8,128)(2,1)} fusion(bf16[32,256,128]{2,1,0:T(8,128)(2,1)S(1)} %bitcast.37, s32[1024]{0:T(1024)S(1)} %pad_clamp_fusion.1), kind=kCustom, calls=%fused_computation | custom fusion | bytes 16777728 | tf_op jit(solution)/shard_map/jit(_take)/gather | solution.py:49
  49.3 17.5 %multiply_bitcast_fusion.1 = f32[128,256,128]{1,2,0:T(8,128)} fusion(bf16[1,1,128,256,256]{4,3,2,1,0:T(8,128)(2,1)} %param.14, f32[128]{0:T(128)S(1)} %get-tuple-element.7, bf16[128,256,128]{2,1,0:T(8,128)(2,1)} %gather_fusion, pred[128]{0:T(512)(128)(4,1)S(1)} %get-tuple-element.8), kind=kOutput, calls=%fused_computation.9 | convolution fusion | flops 2155872256 | bytes 41943680 | tf_op jit(solution)/shard_map/tab,tbf->taf/dot_general | solution.py:50
  66.8 17.4 %copy.15 = f32[128,256,128]{2,1,0:T(8,128)} copy(f32[128,256,128]{1,2,0:T(8,128)} %multiply_bitcast_fusion.1) | data formatting | bytes 33554432 | tf_op jit(solution)/shard_map/mul | solution.py:24
  84.2 4.2 broadcast_in_dim.29
  88.4 38.5 %scatter_fusion = f32[64,256,128]{2,1,0:T(8,128)} fusion(f32[64,256,128]{2,1,0:T(8,128)} %broadcast_in_dim.29, s32[128]{0:T(128)S(1)} %fusion.21, f32[128,256,128]{2,1,0:T(8,128)} %copy.15), kind=kCustom, calls=%fused_computation.2 | custom fusion | flops 4194304 | bytes 50332160 | tf_op jit(solution)/shard_map/scatter-add | solution.py:28
  126.9 0.0 copy-start.2
  126.9 0.0 copy-start.3
  126.9 0.0 copy-start.4
  126.9 6.1 %convert_element_type.39 = bf16[64,256,128]{2,1,0:T(8,128)(2,1)} convert(f32[64,256,128]{2,1,0:T(8,128)} %scatter_fusion) | non-fusion elementwise | flops 2097152 | bytes 12582912 | tf_op jit(solution)/shard_map/convert_element_type | solution.py:51
  133.0 0.0 reduce-scatter.3.cloned.1.call-update
  133.0 0.0 all-gather.2.cloned.1.call-start
  133.1 80.0 %reduce-scatter.3.cloned.1.call-done = bf16[1024,128]{1,0:T(8,128)(2,1)} async-done(((bf16[16384,128]{1,0:T(8,128)(2,1)}), bf16[1024,128]{1,0:T(8,128)(2,1)}) %reduce-scatter.3.cloned.1.call-update) | async-done | bytes 262160 | tf_op jit(solution)/shard_map/reduce_scatter | solution.py:53
  213.1 0.0 copy-done
  213.1 0.0 copy-done.2
  213.1 0.0 copy-done.3
  213.1 2.2 convert_reduce_fusion
  215.3 0.9 convolution_convert_fusion
  216.2 0.0 all-gather.2.cloned.1.call-update
  216.2 0.0 all-reduce.2.cloned.1.call-start
  216.3 0.0 copy-done.4
  216.3 1.9 fusion.26
  218.2 0.0 all-reduce.2.cloned.1.call-update
  218.2 0.2 reduce-scatter.5.cloned.1.call-start
  218.4 54.7 %all-gather.2.cloned.1.call-done = bf16[16384,128]{1,0:T(8,128)(2,1)} async-done(((bf16[1024,128]{1,0:T(8,128)(2,1)}), bf16[16384,128]{1,0:T(8,128)(2,1)}) %all-gather.2.cloned.1.call-update) | async-done | bytes 4194320 | tf_op jit(solution)/shard_map/all_gather | solution.py:63
  273.1 8.8 %gather_fusion.1 = bf16[128,256,128]{2,1,0:T(8,128)(2,1)} fusion(bf16[64,256,128]{2,1,0:T(8,128)(2,1)} %bitcast.38, s32[1024]{0:T(1024)S(1)} %pad_clamp_fusion), kind=kCustom, calls=%fused_computation.1 | custom fusion | bytes 16777728 | tf_op jit(solution)/shard_map/jit(_take)/gather | solution.py:72
  281.9 14.0 %multiply_bitcast_fusion = f32[128,256,128]{1,2,0:T(8,128)} fusion(bf16[1,1,128,256,256]{4,3,2,1,0:T(8,128)(2,1)} %param.14, bf16[128,256,128]{2,1,0:T(8,128)(2,1)} %gather_fusion.1, f32[128]{0:T(128)S(1)} %get-tuple-element.7, pred[128]{0:T(512)(128)(4,1)S(1)} %compare_and_fusion), kind=kOutput, calls=%fused_computation.8 | convolution fusion | flops 2155872256 | bytes 41943680 | tf_op jit(solution)/shard_map/tab,taf->tbf/dot_general | solution.py:75
  295.9 17.4 %copy.17 = f32[128,256,128]{2,1,0:T(8,128)} copy(f32[128,256,128]{1,2,0:T(8,128)} %multiply_bitcast_fusion) | data formatting | bytes 33554432 | tf_op jit(solution)/shard_map/mul | solution.py:24
  313.3 2.4 broadcast_in_dim.32
  315.8 0.0 copy-start.1
  315.8 37.9 %scatter_fusion.1 = f32[32,256,128]{2,1,0:T(8,128)} fusion(f32[32,256,128]{2,1,0:T(8,128)} %broadcast_in_dim.32, s32[128]{0:T(128)S(1)} %fusion.22, f32[128,256,128]{2,1,0:T(8,128)} %copy.17), kind=kCustom, calls=%fused_computation.3 | custom fusion | flops 4194304 | bytes 50332160 | tf_op jit(solution)/shard_map/scatter-add | solution.py:28
  353.7 3.9 convert_element_type.45
  357.6 0.0 reduce-scatter.5.cloned.1.call-update
  357.6 64.8 %psum.15 = f32[128]{0:T(128)S(1)} all-reduce(f32[128]{0:T(128)S(1)} %get-tuple-element.4), channel_id=1, replica_groups=mesh['row'=16,'col'=8] {'row','col'}, use_global_device_ids=true, to_apply=%region_6.7 | all-reduce | flops 128 | bytes 1024 | tf_op jit(solution)/shard_map/psum | solution.py:68
  422.4 0.5 broadcast_multiply_fusion.1
  422.9 0.0 all-reduce.2.cloned.1.call-done
  422.9 1.5 broadcast_multiply_fusion
  424.4 43.3 %reduce-scatter.5.cloned.1.call-done = bf16[1024,128]{1,0:T(8,128)(2,1)} async-done(((bf16[8192,128]{1,0:T(8,128)(2,1)}), bf16[1024,128]{1,0:T(8,128)(2,1)}) %reduce-scatter.5.cloned.1.call-update) | async-done | bytes 262160 | tf_op jit(solution)/shard_map/reduce_scatter | solution.py:80
  467.7 0.0 copy-done.1
  (3 shorter events, 0.0 us)
Async XLA Ops:
  7.2 205.9 %copy-start = (bf16[128,128]{1,0:T(8,128)(2,1)S(1)}, bf16[128,128]{1,0:T(8,128)(2,1)}, u32[]{:S(2)}) copy-start(bf16[128,128]{1,0:T(8,128)(2,1)} %param.9) | copy-start | bytes 98308
  9.8 32.9 %all-to-all-start = ((bf16[8,1024,128]{2,1,0:T(8,128)(2,1)}), bf16[8,1024,128]{2,1,0:T(8,128)(2,1)S(1)}, u32[]{:S(2)}, u32[]{:S(2)}) async-start(bf16[8,1024,128]{2,1,0:T(8,128)(2,1)} %stack.2), calls=%async_computation | async-start | bytes 4194304 | tf_op jit(solution)/shard_map/all_to_all | solution.py:47
  16.6 196.4 %reduce-scatter.3.cloned.1.call-start = ((), (), s32[]{:S(2)}) async-start(), calls=%async_computation.3 | async-start | bytes 4456448 | tf_op jit(solution)/shard_map/reduce_scatter | solution.py:53
  126.9 86.2 %copy-start.2 = (bf16[1024,128]{1,0:T(8,128)(2,1)S(1)}, bf16[1024,128]{1,0:T(8,128)(2,1)}, u32[]{:S(2)}) copy-start(bf16[1024,128]{1,0:T(8,128)(2,1)} %param.11) | copy-start | bytes 786436
  126.9 86.2 %copy-start.3 = (f32[128]{0:T(128)S(1)}, f32[128]{0:T(128)}, u32[]{:S(2)}) copy-start(f32[128]{0:T(128)} %param.10) | copy-start | bytes 1540
  126.9 89.4 %copy-start.4 = (s32[1,1,128]{2,1,0:T(1,128)S(1)}, s32[1,1,128]{2,1,0:T(1,128)}, u32[]{:S(2)}) copy-start(s32[1,1,128]{2,1,0:T(1,128)} %param.12) | copy-start | bytes 1540
  133.0 140.1 %all-gather.2.cloned.1.call-start = ((), (), s32[]{:S(2)}) async-start(), calls=%async_computation.4 | async-start | bytes 4456448 | tf_op jit(solution)/shard_map/all_gather | solution.py:63
  216.2 206.6 %all-reduce.2.cloned.1.call-start = ((), (), s32[]{:S(2)}) async-start(), calls=%async_computation.6 | async-start | bytes 131072 | tf_op jit(solution)/shard_map/psum | solution.py:68
  218.2 249.5 %reduce-scatter.5.cloned.1.call-start = ((), (), s32[]{:S(2)}) async-start(), calls=%async_computation.5 | async-start | bytes 2359296 | tf_op jit(solution)/shard_map/reduce_scatter | solution.py:80
  315.8 151.9 %copy-start.1 = (bf16[128,128]{1,0:T(8,128)(2,1)S(1)}, bf16[128,128]{1,0:T(8,128)(2,1)}, u32[]{:S(2)}) copy-start(bf16[128,128]{1,0:T(8,128)(2,1)} %param.9) | copy-start | bytes 98308
Sparse Core Ops, SparseCore 0:
  133.2 79.8 reduce-scatter.2
  216.4 56.7 all-gather.1
  279.2 136.4 all-reduce.1
  418.5 49.1 reduce-scatter.4
